TPU v7x, 256 devices: a whole 4x4x8 slice. The times are simulated.
256 devices in a mesh: tm: 16 (over x_hi, y, core), rows: 16 (over x_lo, z).
Axes of the slice: x: 4 (x_hi: 2, x_lo: 2; x = x_hi * 2 + x_lo), y: 4, z: 8, core: 2. Of those that a mesh axis runs over, the one named last changes fastest.
Arguments:
- snapshots: bfloat16 [32768, 32768], P('tm', 'rows'), may hold values from -6 to 6
- spod_modes: bfloat16 [64, 2, 4, 32768], P('tm', None, None, 'rows'), may hold values from -0.046875 to 0.046875
- freq_index: int32 [64], replicated, may hold values from 1 to 128, as said below
- seg_offsets: int32 [8192], P('tm'), may hold values from 0 to 2047, as said below
Outputs:
- coefficients: float32 [64, 2, 4, 8192], P('rows', None, None, 'tm')
Inputs may be any that keep to these rules, and one draw needn't show every extreme that they name: Frequency f is bin freq_index[f] of a segment of 256 snapshots; values may repeat. Segment n starts at snapshot (n // 512) * 2048 + seg_offsets[n]; snapshots past the last one count as zeros.
All inputs are finite; a program needn't handle non-finite values.
Results may differ from a plain program's by a relative error of at most 0.0003.
Values may be sent and summed in bfloat16 or wider, within the bound.
A program may use at most 64 MiB of HBM per device.

v0:
```python
import math
import jax
import jax.numpy as jnp
from jax import lax
from jax.sharding import PartitionSpec as P

F = 64
M = 4
L = 256


def hann_weights(distance):
    inside = (distance >= 0) & (distance < L)
    angles = distance.astype(jnp.float32) * (2.0 * math.pi / L)
    values = math.sqrt(8.0 / (3.0 * L)) * (0.5 - 0.5 * jnp.cos(angles))
    return jnp.where(inside, values, 0.0)


def phase_pair(frequency, moments):
    phase_bin = frequency[:, None] * moments[None, :] % L
    angles = phase_bin.astype(jnp.float32) * (2.0 * math.pi / L)
    return (jnp.cos(angles)[:, None, :], jnp.sin(angles)[:, None, :])


def demodulate(projected, frequency, moments):
    cosine, sine_part = phase_pair(frequency, moments)
    real_in = projected[:, 0]
    imag_in = projected[:, 1]
    real_out = cosine * real_in - sine_part * imag_in
    imag_out = -(sine_part * real_in + cosine * imag_in)
    return jnp.stack([real_out, imag_out], 1)


def body(snapshots, spod_modes, freq_index, seg_offsets):
    time_len = snapshots.shape[0]
    tm_pos = lax.axis_index("tm")
    row_pos = lax.axis_index("rows")
    block_rows = lax.all_gather(spod_modes, "tm", axis=0, tiled=True)
    flat_modes = block_rows.reshape(F * 2 * M, block_rows.shape[3])
    partial = lax.dot_general(
        flat_modes, snapshots, (((1,), (1,)), ((), ())), preferred_element_type=jnp.float32
    )
    route = [(i + 1, i) for i in range(lax.axis_size("tm") - 1)]
    behind = lax.ppermute(partial[:, :L], "tm", route)
    moments = tm_pos * time_len + jnp.arange(time_len + L, dtype=jnp.int32)

    def windowed(part, first, length):
        shaped = part.reshape(F, 2, M, length)
        demodulated = demodulate(shaped, freq_index, moments[first : first + length])
        at = first + jnp.arange(length, dtype=jnp.int32)
        weights = hann_weights(at[:, None] - seg_offsets[None, :])
        return lax.dot_general(
            demodulated.reshape(F * 2 * M, length),
            weights,
            (((1,), (0,)), ((), ())),
            precision=lax.Precision.HIGH,
            preferred_element_type=jnp.float32,
        )

    summed = windowed(partial, 0, time_len) + windowed(behind, time_len, L)
    summed = summed.reshape(F, 2, M, seg_offsets.shape[0])
    mine = lax.psum_scatter(summed, "rows", scatter_dimension=0, tiled=True)
    share_len = F // lax.axis_size("rows")
    own_freqs = lax.dynamic_slice_in_dim(freq_index, row_pos * share_len, share_len, 0)
    cosine, sine_part = phase_pair(own_freqs, tm_pos * time_len + seg_offsets)
    env_real = mine[:, 0]
    env_imag = mine[:, 1]
    return jnp.stack(
        [cosine * env_real - sine_part * env_imag, sine_part * env_real + cosine * env_imag], 1
    )


def solution(mesh):
    placed = (P("tm", "rows"), P("tm", None, None, "rows"), P(), P("tm"))
    return jax.shard_map(
        body, mesh=mesh, in_specs=placed, out_specs=P("rows", None, None, "tm"), check_vma=False
    )
```

profile of v0, /device:TPU:8, one launch (start us, length us, event | category | flops | bytes accessed | tf_op | source)
XLA Modules:
  0.0 268.1 jit_solution(8194953738576129666)
XLA Ops:
  6.5 0.7 all-gather.2.cloned.1.call-update
  7.4 1.0 fusion.46
  8.4 2.8 %fusion.41 = (f32[64,2048]{1,0:T(8,128)S(1)}, f32[64,2048]{1,0:T(8,128)S(1)}) fusion(s32[2048]{0:T(1024)S(1)} %slice.36, s32[64]{0:T(128)} %param.6), kind=kLoop, calls=%fused_computation.53 | loop fusion | flops 1835008 | bytes 1057024 | tf_op jit(solution)/shard_map/cos | solution.py:22
  11.1 54.2 %all-gather.2.cloned.1.call-done = bf16[64,2,4,2048]{3,2,1,0:T(4,128)(2,1)} async-done(((bf16[4,2,4,2048]{3,2,1,0:T(4,128)(2,1)}), bf16[64,2,4,2048]{3,2,1,0:T(4,128)(2,1)}) %all-gather.2.cloned.1.call-update) | async-done | bytes 2097168 | tf_op jit(solution)/shard_map/all_gather | solution.py:38
  65.3 2.5 reshape.189
  67.8 7.0 %fusion.64 = f32[512,2048]{1,0:T(8,128)S(1)} fusion(bf16[512,2048]{1,0:T(8,128)(2,1)S(1)} %reshape.189, bf16[2048,2048]{1,0:T(8,128)(2,1)} %param.4), kind=kOutput, calls=%fused_computation.92 | convolution fusion | flops 4294967296 | bytes 14680064 | tf_op jit(solution)/shard_map/dot_general | solution.py:40
  74.8 1.9 copy-done
  76.8 5.2 %reshape.190 = f32[64,2,4,2048]{3,2,1,0:T(4,128)} reshape(f32[512,2048]{1,0:T(8,128)} %copy-done) | data formatting | bytes 8388608 | tf_op jit(solution)/shard_map/reshape | solution.py:48
  82.0 2.9 %multiply_subtract_fusion = (f32[64,1,4,2048]{3,2,1,0:T(4,128)S(1)}, f32[64,1,4,2048]{3,2,1,0:T(4,128)S(1)}) fusion(f32[64,2,4,2048]{3,2,1,0:T(4,128)} %reshape.190, f32[64,2048]{1,0:T(8,128)S(1)} %get-tuple-element.12, f32[64,2048]{1,0:T(8,128)S(1)} %get-tuple-element.11), kind=kLoop, calls=%fused_computation.21 | loop fusion | flops 3670016 | bytes 9437184 | tf_op jit(solution)/shard_map/sub | solution.py:29
  84.9 3.0 %pad_maximum_fusion = f32[64,2,4,2048]{3,2,1,0:T(4,128)} fusion(f32[64,1,4,2048]{3,2,1,0:T(4,128)S(1)} %get-tuple-element.6, f32[64,1,4,2048]{3,2,1,0:T(4,128)S(1)} %get-tuple-element.5), kind=kLoop, calls=%fused_computation | loop fusion | flops 1048576 | bytes 8388608 | tf_op jit(solution)/shard_map/stack | solution.py:31
  87.9 5.3 %reshape.191 = f32[512,2048]{1,0:T(8,128)} reshape(f32[64,2,4,2048]{3,2,1,0:T(4,128)} %pad_maximum_fusion) | data formatting | bytes 8388608 | tf_op jit(solution)/shard_map/reshape | solution.py:53
  93.2 2.8 %collective-permute-start = (f32[512,256]{1,0:T(8,128)S(1)}, f32[512,256]{1,0:T(8,128)S(1)}, u32[]{:S(2)}, u32[]{:S(2)}) collective-permute-start(f32[512,256]{1,0:T(8,128)S(1)} %slice.40), channel_id=1, source_target_pairs={{16,0},{32,16},{48,32},{64,48},{80,64},{96,80},{112,96},{128,112},... | collective-permute-start | bytes 1572872 | tf_op jit(solution)/shard_map/ppermute | solution.py:44
  96.0 20.9 %fusion = f32[512,512]{1,0:T(8,128)S(1)} fusion(f32[512,2048]{1,0:T(8,128)} %reshape.191, s32[512]{0:T(512)S(1)} %copy-done.1), kind=kOutput, calls=%fused_computation.1 | convolution fusion | flops 3231711232 | bytes 5244928 | tf_op jit(solution)/shard_map/dot_general | solution.py:52
  117.0 0.1 reshape.192
  117.1 0.2 multiply_subtract_fusion.1
  117.3 0.1 pad_maximum_fusion.1
  117.4 0.2 reshape.193
  117.6 2.5 convolution_add_fusion
  120.1 1.3 reshape.194
  121.5 0.6 dynamic-slice
  122.8 0.2 fusion.51
  122.9 136.9 %all-reduce.3.cloned.1.call-done = f32[64,2,4,512]{3,2,1,0:T(4,128)} async-done(((f32[64,2,4,512]{3,2,1,0:T(4,128)}), f32[64,2,4,512]{3,2,1,0:T(4,128)}) %all-reduce.3.cloned.1.call-update) | async-done | bytes 1048592
  259.8 0.8 multiply_subtract_fusion.2
  260.6 0.6 pad_maximum_fusion.2
  (18 shorter events, 0.2 us)
Async XLA Ops:
  6.5 58.8 %all-gather.2.cloned.1.call-start = ((), (), s32[]{:S(2)}) async-start(), calls=%async_computation | async-start | bytes 2228224 | tf_op jit(solution)/shard_map/all_gather | solution.py:38
  7.3 252.6 %all-reduce.3.cloned.1.call-start = ((), (), s32[]{:S(2)}) async-start(), calls=%async_computation.1 | async-start | bytes 2097152
  74.8 1.9 copy-start
  87.9 8.1 %copy-start.1 = (s32[512]{0:T(512)S(1)}, s32[512]{0:T(512)}, u32[]{:S(2)}) copy-start(s32[512]{0:T(512)} %param.7) | copy-start | bytes 6148
  93.2 23.7 %collective-permute-start = (f32[512,256]{1,0:T(8,128)S(1)}, f32[512,256]{1,0:T(8,128)S(1)}, u32[]{:S(2)}, u32[]{:S(2)}) collective-permute-start(f32[512,256]{1,0:T(8,128)S(1)} %slice.40), channel_id=1, source_target_pairs={{16,0},{32,16},{48,32},{64,48},{80,64},{96,80},{112,96},{128,112},... | collective-permute-start | bytes 1572872 | tf_op jit(solution)/shard_map/ppermute | solution.py:44
  117.3 4.2 %copy-start.2 = (s32[64]{0:T(128)S(1)}, s32[64]{0:T(128)}, u32[]{:S(2)}) copy-start(s32[64]{0:T(128)} %param.6) | copy-start | bytes 772
  117.3 4.2 %copy-start.3 = (u32[256]{0:T(256)S(1)}, u32[256]{0:T(256)}, u32[]{:S(2)}) copy-start(u32[256]{0:T(256)} %constant.67) | copy-start | bytes 3076
Sparse Core Ops, SparseCore 0:
  10.1 55.1 all-gather.1
  121.6 138.2 all-reduce.2
where the time goes:
time: 269 us; the launch traced here: 268 us
  waiting for transfers between devices  192 us (71%)
  matrix products  30.4 us (11%)
  local copies, waits for them, and re-layouts  17.4 us (6%)
  between operations  14.3 us (5%)
  other arithmetic  11.5 us (4%)
  starting transfers between devices  2.82 us (1%)
    unnamed x3, waiting for transfers between devices  138 us
    all_gather x1, waiting for transfers between devices, body(): block_rows = lax.all_gather(spod_modes, 'tm', axis=0, tiled=True)  54.2 us
    dot_general x2, matrix products, windowed(): lax.dot_general(demodulated.reshape(F * 2 * M, length), weights, (((1,),...  23.4 us
    dot_general x1, matrix products, body(): lax.dot_general(flat_modes, snapshots, (((1,), (1,)), ((), ())), preferre...  6.96 us
    reshape x2, local copies, waits for them, and re-layouts, windowed(): demodulated.reshape(F * 2 * M, length)  5.51 us
  transfers between devices with their start and end apart: 3, of which 2 were waited for; matrix products, arithmetic and copies ran while one was open for 10% of the time, Pallas kernels for 0%

commit v1 on v0

--- a/solution.py
+++ b/solution.py
@@ -35,7 +35,9 @@
     time_len = snapshots.shape[0]
     tm_pos = lax.axis_index("tm")
     row_pos = lax.axis_index("rows")
-    block_rows = lax.all_gather(spod_modes, "tm", axis=0, tiled=True)
+    block_rows = jnp.concatenate(
+        lax.all_to_all(jnp.stack([spod_modes] * lax.axis_size("tm")), "tm", 0, 0), axis=0
+    )
     flat_modes = block_rows.reshape(F * 2 * M, block_rows.shape[3])
     partial = lax.dot_general(
         flat_modes, snapshots, (((1,), (1,)), ((), ())), preferred_element_type=jnp.float32

time: 269 us -> 253 us (0.941)
  waiting for transfers between devices: 192 us -> 166 us
  starting transfers between devices: 2.82 us -> 10.8 us
  local copies, waits for them, and re-layouts: 17.4 us -> 20.1 us
    all_gather x1 -> x0, waiting for transfers between devices: 54.2 us -> none  [body(): block_rows = lax.all_gather(spod_modes, 'tm', axis=0, tiled=True)]
    all_to_all x0 -> x1, waiting for transfers between devices: none -> 24.7 us  [body(): lax.all_to_all(jnp.stack([spod_modes] * lax.axis_size('tm')), 'tm', 0, 0)]
    all_to_all x0 -> x1, starting transfers between devices: none -> 7.39 us  [body(): lax.all_to_all(jnp.stack([spod_modes] * lax.axis_size('tm')), 'tm', 0, 0)]
    another operation x0 -> x2, local copies, waits for them, and re-layouts: none -> 5.33 us  [the longest x1 3.29 us: body(): jnp.stack([spod_modes] * lax.axis_size('tm'))]
    unnamed x3 -> x2, waiting for transfers between devices: 138 us -> 141 us
where the time goes in v1:
time: 253 us; the launch traced here: 252 us
  waiting for transfers between devices  166 us (66%)
  matrix products  31 us (12%)
  local copies, waits for them, and re-layouts  20.1 us (8%)
  between operations  14.2 us (6%)
  starting transfers between devices  10.8 us (4%)
  other arithmetic  10.2 us (4%)
    unnamed x2, waiting for transfers between devices  141 us
    all_to_all x1, waiting for transfers between devices, body(): lax.all_to_all(jnp.stack([spod_modes] * lax.axis_size('tm')), 'tm', 0, 0)  24.7 us
    dot_general x2, matrix products, windowed(): lax.dot_general(demodulated.reshape(F * 2 * M, length), weights, (((1,),...  23.4 us
    dot_general x1, matrix products, body(): lax.dot_general(flat_modes, snapshots, (((1,), (1,)), ((), ())), preferre...  7.63 us
    all_to_all x1, starting transfers between devices, body(): lax.all_to_all(jnp.stack([spod_modes] * lax.axis_size('tm')), 'tm', 0, 0)  7.39 us
    reshape x2, local copies, waits for them, and re-layouts, windowed(): demodulated.reshape(F * 2 * M, length)  5.5 us
    reshape x2, local copies, waits for them, and re-layouts, windowed(): shaped = part.reshape(F, 2, M, length)  5.34 us
  transfers between devices with their start and end apart: 3, of which 2 were waited for; matrix products, arithmetic and copies ran while one was open for 10% of the time, Pallas kernels for 0%

profile of v1, /device:TPU:8, one launch (start us, length us, event | category | flops | bytes accessed | tf_op | source)
XLA Modules:
  0.0 252.5 jit_solution(17369444606605512372)
XLA Ops:
  6.5 3.3 %stack.8 = bf16[16,4,2,4,2048]{4,3,2,1,0:T(4,128)(2,1)} broadcast(bf16[4,2,4,2048]{3,2,1,0:T(4,128)(2,1)} %param.5), dimensions={1,2,3,4} | broadcast | bytes 2228224 | tf_op jit(solution)/shard_map/stack | solution.py:39
  9.8 7.4 %all-to-all-start = ((bf16[16,4,2,4,2048]{4,3,2,1,0:T(4,128)(2,1)}), bf16[16,4,2,4,2048]{4,3,2,1,0:T(4,128)(2,1)S(1)}, u32[]{:S(2)}, u32[]{:S(2)}) async-start(bf16[16,4,2,4,2048]{4,3,2,1,0:T(4,128)(2,1)} %stack.8), calls=%async_computation | async-start | bytes 4194304 | tf_op jit(solution)/shard_map/all_to_all | solution.py:39
  17.3 0.3 fusion.46
  17.7 2.1 fusion.41
  19.8 24.7 %all-to-all-done = bf16[16,4,2,4,2048]{4,3,2,1,0:T(4,128)(2,1)S(1)} async-done(((bf16[16,4,2,4,2048]{4,3,2,1,0:T(4,128)(2,1)}), bf16[16,4,2,4,2048]{4,3,2,1,0:T(4,128)(2,1)S(1)}, u32[]{:S(2)}, u32[]{:S(2)}) %all-to-all-start) | async-done | bytes 2097184 | tf_op jit(solution)/shard_map/all_to_all | solution.py:39
  44.5 2.0 reshape_reshape.3
  46.6 7.6 %fusion.64 = f32[512,2048]{1,0:T(8,128)S(1)} fusion(bf16[512,2048]{1,0:T(8,128)(2,1)} %reshape_reshape.3, bf16[2048,2048]{1,0:T(8,128)(2,1)} %param.4), kind=kOutput, calls=%fused_computation.92 | convolution fusion | flops 4294967296 | bytes 14680064 | tf_op jit(solution)/shard_map/dot_general | solution.py:42
  54.2 1.9 copy-done
  56.2 5.2 %reshape.188 = f32[64,2,4,2048]{3,2,1,0:T(4,128)} reshape(f32[512,2048]{1,0:T(8,128)} %copy-done) | data formatting | bytes 8388608 | tf_op jit(solution)/shard_map/reshape | solution.py:50
  61.4 2.9 %multiply_subtract_fusion = (f32[64,1,4,2048]{3,2,1,0:T(4,128)S(1)}, f32[64,1,4,2048]{3,2,1,0:T(4,128)S(1)}) fusion(f32[64,2,4,2048]{3,2,1,0:T(4,128)} %reshape.188, f32[64,2048]{1,0:T(8,128)S(1)} %get-tuple-element.12, f32[64,2048]{1,0:T(8,128)S(1)} %get-tuple-element.11), kind=kLoop, calls=%fused_computation.21 | loop fusion | flops 3670016 | bytes 9437184 | tf_op jit(solution)/shard_map/sub | solution.py:29
  64.2 3.0 %pad_maximum_fusion = f32[64,2,4,2048]{3,2,1,0:T(4,128)} fusion(f32[64,1,4,2048]{3,2,1,0:T(4,128)S(1)} %get-tuple-element.6, f32[64,1,4,2048]{3,2,1,0:T(4,128)S(1)} %get-tuple-element.5), kind=kLoop, calls=%fused_computation | loop fusion | flops 1048576 | bytes 8388608 | tf_op jit(solution)/shard_map/stack | solution.py:31
  67.3 5.3 %reshape.189 = f32[512,2048]{1,0:T(8,128)} reshape(f32[64,2,4,2048]{3,2,1,0:T(4,128)} %pad_maximum_fusion) | data formatting | bytes 8388608 | tf_op jit(solution)/shard_map/reshape | solution.py:55
  72.6 3.4 %collective-permute-start = (f32[512,256]{1,0:T(8,128)S(1)}, f32[512,256]{1,0:T(8,128)S(1)}, u32[]{:S(2)}, u32[]{:S(2)}) collective-permute-start(f32[512,256]{1,0:T(8,128)S(1)} %slice.40), channel_id=1, source_target_pairs={{16,0},{32,16},{48,32},{64,48},{80,64},{96,80},{112,96},{128,112},... | collective-permute-start | bytes 1572872 | tf_op jit(solution)/shard_map/ppermute | solution.py:46
  76.0 20.9 %fusion = f32[512,512]{1,0:T(8,128)S(1)} fusion(f32[512,2048]{1,0:T(8,128)} %reshape.189, s32[512]{0:T(512)S(1)} %copy-done.1), kind=kOutput, calls=%fused_computation.1 | convolution fusion | flops 3231711232 | bytes 5244928 | tf_op jit(solution)/shard_map/dot_general | solution.py:54
  96.9 0.1 reshape.190
  97.1 0.2 multiply_subtract_fusion.1
  97.4 0.2 reshape.191
  97.6 2.5 convolution_add_fusion
  100.1 1.3 reshape.192
  101.5 0.6 dynamic-slice
  102.7 0.2 fusion.51
  102.9 141.3 %all-reduce.3.cloned.1.call-done = f32[64,2,4,512]{3,2,1,0:T(4,128)} async-done(((f32[64,2,4,512]{3,2,1,0:T(4,128)}), f32[64,2,4,512]{3,2,1,0:T(4,128)}) %all-reduce.3.cloned.1.call-update) | async-done | bytes 1048592
  244.2 0.8 multiply_subtract_fusion.2
  245.0 0.6 pad_maximum_fusion.2
  (18 shorter events, 0.3 us)
Async XLA Ops:
  6.5 10.8 %copy-start.2 = (s32[64]{0:T(128)S(1)}, s32[64]{0:T(128)}, u32[]{:S(2)}) copy-start(s32[64]{0:T(128)} %param.6) | copy-start | bytes 772
  9.8 34.7 %all-to-all-start = ((bf16[16,4,2,4,2048]{4,3,2,1,0:T(4,128)(2,1)}), bf16[16,4,2,4,2048]{4,3,2,1,0:T(4,128)(2,1)S(1)}, u32[]{:S(2)}, u32[]{:S(2)}) async-start(bf16[16,4,2,4,2048]{4,3,2,1,0:T(4,128)(2,1)} %stack.8), calls=%async_computation | async-start | bytes 4194304 | tf_op jit(solution)/shard_map/all_to_all | solution.py:39
  17.2 226.9 %all-reduce.3.cloned.1.call-start = ((), (), s32[]{:S(2)}) async-start(), calls=%async_computation.1 | async-start | bytes 2097152
  54.2 1.9 copy-start
  67.3 8.7 %copy-start.1 = (s32[512]{0:T(512)S(1)}, s32[512]{0:T(512)}, u32[]{:S(2)}) copy-start(s32[512]{0:T(512)} %param.7) | copy-start | bytes 6148
  72.6 24.3 %collective-permute-start = (f32[512,256]{1,0:T(8,128)S(1)}, f32[512,256]{1,0:T(8,128)S(1)}, u32[]{:S(2)}, u32[]{:S(2)}) collective-permute-start(f32[512,256]{1,0:T(8,128)S(1)} %slice.40), channel_id=1, source_target_pairs={{16,0},{32,16},{48,32},{64,48},{80,64},{96,80},{112,96},{128,112},... | collective-permute-start | bytes 1572872 | tf_op jit(solution)/shard_map/ppermute | solution.py:46
  97.2 4.2 %copy-start.3 = (u32[256]{0:T(256)S(1)}, u32[256]{0:T(256)}, u32[]{:S(2)}) copy-start(u32[256]{0:T(256)} %constant.67) | copy-start | bytes 3076
Sparse Core Ops, SparseCore 0:
  101.5 142.6 all-reduce.2
